TPU v7x, 128 devices: a whole 4x4x4 slice. The times are simulated.
128 devices in a mesh: virt: 16 (over y, z), occ: 8 (over x, core).
Axes of the slice: x: 4, y: 4, z: 4, core: 2. Of those that a mesh axis runs over, the one named last changes fastest.
Arguments:
- amplitudes: bfloat16 [64, 1024, 14400], P(None, ('virt', 'occ')), may hold values from -6 to 6
- integrals: bfloat16 [1024, 120, 960], P(('virt', 'occ')), may hold values from -0.046875 to 0.046875
- a_irrep: int32 [64], replicated, may hold values from 0 to 7
- b_irrep: int32 [8], replicated, may hold values from 0 to 7
- virt_irrep: int32 [1024], replicated, may hold values from 0 to 7, as said below
- occ_irrep: int32 [120], replicated, may hold values from 0 to 7, as said below
Outputs:
- cycle_term: float32 [64, 120, 960], P('virt', 'occ')
Inputs may be any that keep to these rules, and one draw needn't show every extreme that they name: `virt_irrep`: nondecreasing along the 1024 virtuals (orbitals ordered by irrep, ragged blocks, some possibly empty); the first is 0 and the last 7. `occ_irrep`: nondecreasing along the 120 occupied orbitals (ragged blocks, some possibly empty); the first is 0 and the last 7.
All inputs are finite; a program needn't handle non-finite values.
Results may differ from a plain program's by a relative error of at most 0.0003.
Values may be sent and summed in bfloat16 or wider, within the bound.
No kernel may reach another device: no remote copies, remote signals or barrier semaphores. Data moves between devices by JAX's collectives and lax.ppermute only.
A program may use at most 192 MiB of HBM per device.

v0:
```python
import jax
import jax.numpy as jnp
from jax import lax
from jax.sharding import PartitionSpec as P


def pair_symmetry(left_labels, right_labels):
    return jnp.bitwise_xor(left_labels[:, None], right_labels[None, :])


def masked_amplitudes(amp_block, a_labels, e_labels, occ_irrep):
    occ_pairs = pair_symmetry(occ_irrep, occ_irrep).reshape(-1)
    keep_amp = pair_symmetry(a_labels, e_labels)[:, :, None] == occ_pairs[None, None, :]
    masked = jnp.where(keep_amp, amp_block, jnp.zeros((), amp_block.dtype))
    orbitals = occ_irrep.shape[0]
    return masked.reshape(amp_block.shape[0], amp_block.shape[1], orbitals, orbitals)


def contract(masked, int_block):
    return jnp.einsum("aeim,emx->aix", masked, int_block, preferred_element_type=jnp.float32)


def symmetric_part(partial_value, a_labels, i_labels, b_irrep, occ_irrep):
    row_sym = pair_symmetry(a_labels, i_labels)
    col_sym = pair_symmetry(b_irrep, occ_irrep).reshape(-1)
    keep_out = row_sym[:, :, None] == col_sym[None, None, :]
    return jnp.where(keep_out, partial_value, jnp.zeros((), partial_value.dtype))


def on_device(amplitudes, integrals, a_irrep, b_irrep, virt_irrep, occ_irrep):
    virt_count = lax.axis_size("virt")
    occ_count = lax.axis_size("occ")
    virt_index = lax.axis_index("virt")
    occ_index = lax.axis_index("occ")
    local_e = amplitudes.shape[1]
    orbitals = occ_irrep.shape[0]
    i_share = orbitals // occ_count
    a_share = amplitudes.shape[0] // virt_count
    a_labels = lax.dynamic_slice_in_dim(a_irrep, virt_index * a_share, a_share, 0)
    cycle_amp = lax.all_to_all(amplitudes, "virt", split_axis=0, concat_axis=1, tiled=True)
    e_table = virt_irrep.reshape(virt_count, occ_count, local_e)
    e_labels = lax.dynamic_index_in_dim(e_table, occ_index, 1, keepdims=False).reshape(-1)
    masked = masked_amplitudes(cycle_amp, a_labels, e_labels, occ_irrep)
    partial_value = contract(masked, lax.all_gather(integrals, "virt", axis=0, tiled=True))
    shares = lax.psum_scatter(partial_value, "occ", scatter_dimension=1, tiled=True)
    i_labels = lax.dynamic_slice_in_dim(occ_irrep, occ_index * i_share, i_share, 0)
    return symmetric_part(shares, a_labels, i_labels, b_irrep, occ_irrep)


def solution(mesh):
    placed = (P(None, ("virt", "occ"), None), P(("virt", "occ"), None, None), P(), P(), P(), P())
    return jax.shard_map(
        on_device, mesh=mesh, in_specs=placed, out_specs=P("virt", "occ", None), check_vma=False
    )
```

profile of v0, /device:TPU:0, one launch (start us, length us, event | category | flops | bytes accessed | tf_op | source)
XLA Modules:
  0.0 526.8 jit_solution(528032864982171976)
XLA Ops:
  6.5 0.0 copy-start.1
  6.5 0.0 copy-start.3
  6.5 0.0 copy-start
  6.5 0.0 all-gather.2.cloned.1.call-start
  6.5 0.7 all-gather.2.cloned.1.call-update
  7.3 8.2 %all-to-all-start = ((bf16[64,8,14400]{2,1,0:T(8,128)(2,1)}), bf16[64,8,14400]{2,1,0:T(8,128)(2,1)}, u32[]{:S(2)}, u32[]{:S(2)}) async-start(bf16[64,8,14400]{2,1,0:T(8,128)(2,1)} %param.6), calls=%async_computation | async-start | bytes 29622272 | tf_op jit(solution)/shard_map/all_to_all | solution.py:40
  15.5 0.0 all-reduce.3.cloned.1.call-start
  15.5 0.0 copy-done.1
  15.5 0.1 reshape.91
  15.7 0.1 xor.81
  15.7 0.0 copy-done.3
  15.8 0.1 dynamic_slice.10
  15.8 0.1 broadcast_xor_fusion.3
  15.9 0.0 copy-done
  15.9 0.1 broadcast_xor_fusion
  16.0 277.9 %all-to-all-done = bf16[64,8,14400]{2,1,0:T(8,128)(2,1)} async-done(((bf16[64,8,14400]{2,1,0:T(8,128)(2,1)}), bf16[64,8,14400]{2,1,0:T(8,128)(2,1)}, u32[]{:S(2)}, u32[]{:S(2)}) %all-to-all-start) | async-done | bytes 14745632 | tf_op jit(solution)/shard_map/all_to_all | solution.py:40
  293.9 12.6 %copy.19 = bf16[16,4,8,14400]{3,2,0,1:T(8,128)(2,1)} copy(bf16[16,4,8,14400]{3,2,1,0:T(8,128)(2,1)} %bitcast) | data formatting | bytes 29491200 | tf_op jit(solution)/shard_map/all_to_all | solution.py:40
  306.6 27.9 %all_to_all.16 = bf16[4,128,120,120]{3,2,1,0:T(8,128)(2,1)} reshape(bf16[4,16,8,14400]{3,2,1,0:T(8,128)(2,1)} %bitcast.15) | data formatting | bytes 29491200 | tf_op jit(solution)/shard_map/all_to_all | solution.py:40
  334.5 0.0 copy-start.2
  334.5 75.7 %all-gather.2.cloned.1.call-done = bf16[128,120,960]{2,1,0:T(8,128)(2,1)} async-done(((bf16[8,120,960]{2,1,0:T(8,128)(2,1)}), bf16[128,120,960]{2,1,0:T(8,128)(2,1)}) %all-gather.2.cloned.1.call-update) | async-done | bytes 29491216 | tf_op jit(solution)/shard_map/all_gather | solution.py:44
  410.2 26.7 %fusion.5 = f32[4,120,960]{2,1,0:T(8,128)S(1)} fusion(bf16[128,120,960]{2,1,0:T(8,128)(2,1)} %all-gather.2.cloned.1.call-done, bf16[4,128,120,120]{3,2,1,0:T(8,128)(2,1)} %all_to_all.16, s32[120,120]{1,0:T(8,128)S(1)} %broadcast_xor_fusion, s32[4,128]{1,0:T(4,128)S(1)} %broadcast_xor_fusion.3), kind=kOutput, calls=%fused_computation.7 | convolution fusion | flops 14170521600 | bytes 46139648 | tf_op jit(solution)/shard_map/aeim,emx->aix/dot_general | solution.py:20
  436.9 2.5 copy.16
  439.4 0.0 all-reduce.3.cloned.1.call-update
  439.4 0.1 dynamic_slice.11
  439.5 0.0 copy-done.2
  439.5 0.1 broadcast_xor_fusion.2
  439.6 0.1 xor.79
  439.6 0.0 copy-done.4
  439.7 0.6 dynamic-slice
  440.9 0.1 broadcast_xor_fusion.1
  441.0 77.3 %all-reduce.3.cloned.1.call-done = f32[4,120,960]{2,0,1:T(4,128)} async-done(((f32[4,120,960]{2,0,1:T(4,128)}), f32[4,120,960]{2,0,1:T(4,128)}) %all-reduce.3.cloned.1.call-update) | async-done | bytes 1843216
  518.2 1.8 dynamic-slice_select_fusion
  (2 shorter events, 0.0 us)
Async XLA Ops:
  6.5 9.0 %copy-start.1 = (s32[1024]{0:T(1024)S(1)}, s32[1024]{0:T(1024)}, u32[]{:S(2)}) copy-start(s32[1024]{0:T(1024)} %param.10) | copy-start | bytes 12292
  6.5 9.2 %copy-start.3 = (s32[64]{0:T(128)S(1)}, s32[64]{0:T(128)}, u32[]{:S(2)}) copy-start(s32[64]{0:T(128)} %param.8) | copy-start | bytes 772
  6.5 9.4 %copy-start = (s32[120]{0:T(128)S(1)}, s32[120]{0:T(128)}, u32[]{:S(2)}) copy-start(s32[120]{0:T(128)} %param.11) | copy-start | bytes 1444
  6.5 403.7 %all-gather.2.cloned.1.call-start = ((), (), s32[]{:S(2)}) async-start(), calls=%async_computation.1 | async-start | bytes 33423360 | tf_op jit(solution)/shard_map/all_gather | solution.py:44
  7.3 286.7 %all-to-all-start = ((bf16[64,8,14400]{2,1,0:T(8,128)(2,1)}), bf16[64,8,14400]{2,1,0:T(8,128)(2,1)}, u32[]{:S(2)}, u32[]{:S(2)}) async-start(bf16[64,8,14400]{2,1,0:T(8,128)(2,1)} %param.6), calls=%async_computation | async-start | bytes 29622272 | tf_op jit(solution)/shard_map/all_to_all | solution.py:40
  15.5 502.8 %all-reduce.3.cloned.1.call-start = ((), (), s32[]{:S(2)}) async-start(), calls=%async_computation.2 | async-start | bytes 3932160
  334.5 105.0 %copy-start.2 = (s32[8]{0:T(128)S(1)}, s32[8]{0:T(128)}, u32[]{:S(2)}) copy-start(s32[8]{0:T(128)} %param.9) | copy-start | bytes 100
  334.5 105.2 %copy-start.4 = (u32[128]{0:T(128)S(1)}, u32[128]{0:T(128)}, u32[]{:S(2)}) copy-start(u32[128]{0:T(128)} %constant.32) | copy-start | bytes 1540
Sparse Core Ops, SparseCore 0:
  9.6 400.5 all-gather.1
  439.5 78.6 all-reduce.2
where the time goes:
time: 528 us; the launch traced here: 527 us
  waiting for transfers between devices  432 us (82%)
  local copies, waits for them, and re-layouts  44.1 us (8%)
  matrix products  26.7 us (5%)
  between operations  14.1 us (3%)
  starting transfers between devices  8.23 us (2%)
    all_to_all x1, waiting for transfers between devices, on_device(): lax.all_to_all(amplitudes, 'virt', split_axis=0, concat_axis=1, tiled=True)  278 us
    unnamed x3, waiting for transfers between devices  78 us
    all_gather x1, waiting for transfers between devices, on_device(): lax.all_gather(integrals, 'virt', axis=0, tiled=True)  75.7 us
    all_to_all x2, local copies, waits for them, and re-layouts, on_device(): lax.all_to_all(amplitudes, 'virt', split_axis=0, concat_axis=1, tiled=True)  40.5 us
    dot_general x1, matrix products, contract(): jnp.einsum('aeim,emx->aix', masked, int_block, preferred_element_type=jnp...  26.7 us
  transfers between devices with their start and end apart: 3, of which 3 were waited for; matrix products, arithmetic and copies ran while one was open for 3% of the time, Pallas kernels for 0%

commit v1 on v0

v1 whole, which is shorter than its diff:
```python
import jax
import jax.numpy as jnp
from jax import lax
from jax.experimental import pallas as pl
from jax.experimental.pallas import tpu as pltpu
from jax.sharding import Mesh, PartitionSpec as P

O = 120
BJ = 960
AW = 64
CAP = 255
LANES = 256
VMEM = 60 * 1024 * 1024


def quantized(rows):
    largest = jnp.max(jnp.abs(rows), axis=-1, keepdims=True)
    power = jnp.clip(jnp.floor(jnp.log2(largest * 1.001)) + 1.0, -100.0, 126.0)
    codes = jnp.round(rows * jnp.exp2(15.0 - power))
    lane = lax.broadcasted_iota(jnp.int32, rows.shape, rows.ndim - 1)
    return jnp.where(lane == LANES - 1, power, codes)

def contract_kernel(place, a_s, b_s, virt_s, occ_s, amp, ints, tail, occ_row, keep, send,
                    buf, wbuf, weights0, weights1, stage, labels, left0, left1, acc0, acc1, codes, sems, wsem, osem):
    device = place[0]; core = lax.rem(device, 2); first = place[1]
    wcopy = pltpu.make_async_copy(ints, wbuf, wsem)
    wcopy.start()
    def piece(q, g):
        start = 1920 * g + 512 * q
        size = 384 if q == 3 else 512
        if g == 7:
            if q >= 2: return None
            size = min(size, 14336 - start)
        return pltpu.make_async_copy(amp.at[:, :, pl.ds(start, size)], buf.at[:, :, pl.ds(start, size)], sems.at[q, g])
    copies = [[c for g in range(8) if (c := piece(q, g)) is not None] for q in range(4)]
    for q in range(4):
        for c in copies[q]: c.start()
    buf[:, :, 14336:] = tail[...]
    sub = lax.broadcasted_iota(jnp.int32, (8, 128), 0)
    e_label = jnp.zeros((8, 128), jnp.int32)
    e_scalars = [virt_s[device * 8 + e] for e in range(8)]
    for e in range(8):
        e_label = jnp.where(sub == e, e_scalars[e], e_label)
    def set_label(a, c):
        labels[a] = (e_label ^ a_s[a]).astype(labels.dtype)
        return c
    lax.fori_loop(0, AW, set_label, 0)
    turned = jnp.broadcast_to(occ_row[...], (128, 128))
    diag = lax.broadcasted_iota(jnp.int32, (128, 128), 0) == lax.broadcasted_iota(jnp.int32, (128, 128), 1)
    occ_col = jnp.sum(jnp.where(diag, turned, 0), axis=1, keepdims=True)[:O]
    x_lane = lax.broadcasted_iota(jnp.int32, (128, BJ), 1)
    m_sub = lax.broadcasted_iota(jnp.int32, (128, BJ), 0)
    x_row = lax.broadcasted_iota(jnp.int32, (1, BJ), 1)
    hit = jnp.zeros((128, BJ), jnp.bool_)
    occ_lane = jnp.zeros((1, BJ), jnp.int32)
    b_row = jnp.zeros((1, BJ), jnp.int32)
    for b in range(8):
        hit = hit | (x_lane - b * O == m_sub)
        b_row = jnp.where((x_row >= b * O), b_s[b], b_row)
    hit = hit & (m_sub < O)
    occ128 = jnp.sum(jnp.where(diag, turned, 0), axis=1, keepdims=True)
    class_row = jnp.sum(jnp.where(hit, occ128, 0), axis=0, keepdims=True) ^ b_row
    picks = []
    for part in range(8):
        shape = (O, BJ)
        mine = lax.broadcasted_iota(jnp.int32, shape, 0) + part * O
        other = lax.broadcasted_iota(jnp.int32, shape, 1)
        same = ((occ_col ^ b_s[part]) == class_row) & (other < mine)
        rank = jnp.sum(jnp.where(same, 1.0, 0.0), axis=1, keepdims=True) - first.astype(jnp.float32)
        slot = lax.broadcasted_iota(jnp.int32, (O, LANES), 1).astype(jnp.float32)
        chosen = (rank == slot) & (slot < CAP)
        picks.append(jnp.where(chosen, 1.0, 0.0))
    pick = jnp.concatenate(picks, axis=0).astype(jnp.bfloat16)
    wcopy.wait()
    for e in range(8):
        kept = jnp.where((occ_col ^ e_scalars[e]) == class_row, wbuf[e].astype(jnp.float32), 0.0)
        packed = jnp.dot(kept.astype(jnp.bfloat16), pick, preferred_element_type=jnp.float32)
        whole = jnp.concatenate([packed, jnp.zeros((128 - O, LANES), jnp.float32)], axis=0)
        weights0[e] = jnp.concatenate([whole, whole], axis=0).astype(jnp.bfloat16)
        weights1[e] = jnp.concatenate([whole[8:], whole, whole[:8]], axis=0).astype(jnp.bfloat16)

    lane = lax.broadcasted_iota(jnp.int32, (AW, 8, 128), 2)
    lane2 = lax.broadcasted_iota(jnp.int32, (8, 128), 1)
    occ8 = jnp.where(lane2 < O, jnp.broadcast_to(occ_row[...], (8, 128)), 64)

    def build(k, left):
        rolled = pltpu.roll(occ8, lax.rem(128 - 8 * k + 128, 128), axis=1)
        for g in range(8):
            tile = 15 * g + k
            now = buf[:, :, pl.ds(pl.multiple_of(jnp.minimum(tile, 112) * 128, 128), 128)]
            before = buf[:, :, pl.ds(pl.multiple_of(jnp.clip(tile - 1, 0, 112) * 128, 128), 128)]
            pair = (rolled ^ occ_s[jnp.minimum(16 * g + k, O - 1)])[None]
            merged = jnp.where(lane < O - 8 * k, now.astype(jnp.float32), before.astype(jnp.float32))
            merged = jnp.where(labels[...] == pair, merged, 0.0)
            for a in range(AW):
                stage[pl.ds(g * 520 + a, 8, stride=65), :] = merged[a]
            for e in range(8):
                rows = stage[pl.ds(g * 520 + 65 * e, 64), :]
                left[g * 64:(g + 1) * 64, e * 128:(e + 1) * 128] = rows.astype(jnp.bfloat16)

    def multiply(k, left, weights, acc):
        right = weights[:, pl.ds(pl.multiple_of(lax.div(k, 2) * 16, 16), 128), :]
        acc[...] = jnp.dot(left[...], right.reshape(1024, LANES), preferred_element_type=jnp.float32)

    def emit(k, acc):
        for g in range(8):
            i = 16 * g + k
            block = lax.div(i, 15)
            inner = i - block * 15
            ok = (k >= 0) & (i < O)
            x = jnp.where(ok, lax.div(block, 2), 4)
            inner = jnp.where(ok, inner, 0)
            slot = lax.rem(block + core, 2)
            codes[jnp.where(ok, slot, 0), x, inner] = quantized(acc[g * 64:(g + 1) * 64, :]).astype(jnp.int16)

    def wait(q):
        for c in copies[q]: c.wait()
    wait(0)
    acc1[...] = jnp.zeros_like(acc1)
    build(jnp.int32(0), left0)
    def turn(kk, carry):
        for q in range(1, 4):
            @pl.when(kk == 2 * q - 1)
            def _():
                wait(q)
        k = 2 * kk
        multiply(k, left0, weights0, acc0)
        build(k + 1, left1)
        emit(k - 1, acc1)
        multiply(k + 1, left1, weights1, acc1)
        build(jnp.minimum(k + 2, 15), left0)
        emit(k, acc0)
        return carry
    lax.fori_loop(0, 8, turn, 0)
    emit(jnp.int32(15), acc1)
    o1 = pltpu.make_async_copy(codes.at[0, pl.ds(0, 4)], keep, osem.at[0]); o1.start()
    o2 = pltpu.make_async_copy(codes.at[1, pl.ds(0, 4)], send, osem.at[1]); o2.start()
    o1.wait(); o2.wait()

def contract(place, a, b, virt, occ, amp, ints):
    any_ = pl.BlockSpec(memory_space=pl.ANY)
    vm = pl.BlockSpec(memory_space=pltpu.VMEM)
    sm = pl.BlockSpec(memory_space=pltpu.SMEM)
    occ_row = jnp.pad(occ, (0, 8))[None]
    return pl.pallas_call(
        contract_kernel,
        grid=(1,),
        in_specs=[sm] * 5 + [any_, any_, pl.BlockSpec((AW, 8, 128), lambda s: (0, 0, 112)), vm],
        out_specs=[any_, any_],
        scratch_shapes=[
            pltpu.VMEM((AW, 8, 113 * 128), jnp.bfloat16),
            pltpu.VMEM((8, O, BJ), jnp.bfloat16),
            pltpu.VMEM((8, 256, LANES), jnp.bfloat16),
            pltpu.VMEM((8, 256, LANES), jnp.bfloat16),
            pltpu.VMEM((4096+64, 128), jnp.float32),
            pltpu.VMEM((AW, 8, 128), jnp.int32),
            pltpu.VMEM((512, 1024), jnp.bfloat16),
            pltpu.VMEM((512, 1024), jnp.bfloat16),
            pltpu.VMEM((512, LANES), jnp.float32),
            pltpu.VMEM((512, LANES), jnp.float32),
            pltpu.VMEM((2, 5, 15, AW, LANES), jnp.int16),
            pltpu.SemaphoreType.DMA((4, 8)),
            pltpu.SemaphoreType.DMA,
            pltpu.SemaphoreType.DMA((2,)),
        ],
        out_shape=[
            jax.ShapeDtypeStruct((4, 15, AW, LANES), jnp.int16),
            jax.ShapeDtypeStruct((4, 15, AW, LANES), jnp.int16),
        ],
        compiler_params=pltpu.CompilerParams(vmem_limit_bytes=VMEM),
        name="contract",
    )(place, a, b, virt, occ, amp, ints, amp, occ_row)


def combined(one, two):
    one, two = one.astype(jnp.float32), two.astype(jnp.float32)
    power_one, power_two = one[..., LANES - 1 :], two[..., LANES - 1 :]
    power = jnp.maximum(power_one, power_two) + 1.0
    total = jnp.round(one * jnp.exp2(power_one - power) + two * jnp.exp2(power_two - power))
    lane = lax.broadcasted_iota(jnp.int32, one.shape, one.ndim - 1)
    return jnp.where(lane == LANES - 1, power, total)


def merge_kernel(own, came, out):
    for quad in range(4):
        sums = []
        for inner in range(4 * quad, min(4 * quad + 4, 15)):
            sums.append(combined(own[0, inner], came[0, inner]).reshape(8, 8, LANES))
        if quad == 3:
            sums.append(jnp.zeros_like(sums[0]))
        for half in range(2):
            rows = jnp.concatenate([s[:, 4 * half : 4 * half + 4] for s in sums], axis=1)
            out[:, half, 0, 16 * quad : 16 * quad + 16, :] = rows.astype(jnp.int16)


def merge(own, came):
    out = pl.pallas_call(
        merge_kernel,
        grid=(4,),
        in_specs=[pl.BlockSpec((1, 15, AW, LANES), lambda x: (x, 0, 0, 0))] * 2,
        out_specs=pl.BlockSpec((8, 2, 1, 64, LANES), lambda x: (0, 0, x, 0, 0)),
        out_shape=jax.ShapeDtypeStruct((8, 2, 4, 64, LANES), jnp.int16),
        compiler_params=pltpu.CompilerParams(vmem_limit_bytes=VMEM),
        name="merge",
    )(own, came)
    return out.reshape(64, 64, LANES)


def table_kernel(first, class_row, class_col, table):
    shape = (O, BJ)
    rank = jnp.zeros((1, BJ), jnp.float32)
    for part in range(8):
        before = lax.broadcasted_iota(jnp.int32, shape, 0) + part * O < lax.broadcasted_iota(jnp.int32, shape, 1)
        same = (class_col[part * O : (part + 1) * O, :] == class_row[...]) & before
        rank = rank + jnp.sum(jnp.where(same, 1.0, 0.0), axis=0, keepdims=True)
    slot = lax.broadcasted_iota(jnp.int32, (LANES, BJ), 0).astype(jnp.float32)
    chosen = (rank - first[0].astype(jnp.float32) == slot) & (slot < CAP)
    table[...] = jnp.where(chosen, 1.0, 0.0).astype(jnp.bfloat16)


def make_table(first, class_row, class_col):
    vm = pl.BlockSpec(memory_space=pltpu.VMEM)
    return pl.pallas_call(
        table_kernel,
        in_specs=[pl.BlockSpec(memory_space=pltpu.SMEM), vm, vm],
        out_specs=vm,
        out_shape=jax.ShapeDtypeStruct((LANES, BJ), jnp.bfloat16),
        compiler_params=pltpu.CompilerParams(vmem_limit_bytes=VMEM),
        name="table",
    )(first, class_row, class_col)


BATCH = 32


def expand_kernel(came, table, class_row, row_class, out, total):
    step = pl.program_id(0)
    part = jnp.zeros((64, LANES), jnp.float32)
    for n in range(BATCH):
        values = came[n].astype(jnp.float32)
        part = part + values * jnp.exp2(values[:, LANES - 1 :] - 15.0)

    @pl.when(step == 0)
    def _():
        total[...] = part

    @pl.when(step > 0)
    def _():
        total[...] = total[...] + part

    @pl.when(step == pl.num_programs(0) - 1)
    def _():
        lane = lax.broadcasted_iota(jnp.int32, (64, LANES), 1)
        value = jnp.where(lane == LANES - 1, 0.0, total[...])
        high = value.astype(jnp.bfloat16)
        rest = value - high.astype(jnp.float32)
        middle = rest.astype(jnp.bfloat16)
        low = (rest - middle.astype(jnp.float32)).astype(jnp.bfloat16)
        parts = jnp.concatenate([high, middle, low], axis=0)
        spread = jnp.dot(parts, table[...], preferred_element_type=jnp.float32)
        spread = spread[:64] + (spread[64:128] + spread[128:])
        out[...] = jnp.where(row_class[...] == class_row[...], spread, 0.0)[:60]


def expand(came, table, class_row, row_class):
    whole = lambda *shape: pl.BlockSpec(shape, lambda n: (0,) * len(shape))
    return pl.pallas_call(
        expand_kernel,
        grid=(64 // BATCH,),
        in_specs=[
            pl.BlockSpec((BATCH, 64, LANES), lambda n: (n, 0, 0)),
            whole(LANES, BJ),
            whole(1, BJ),
            whole(64, 1),
        ],
        out_specs=whole(60, BJ),
        out_shape=jax.ShapeDtypeStruct((60, BJ), jnp.float32),
        scratch_shapes=[pltpu.VMEM((64, LANES), jnp.float32)],
        compiler_params=pltpu.CompilerParams(vmem_limit_bytes=VMEM),
        name="expand",
    )(came, table, class_row, row_class)


def on_device(amplitudes, integrals, a_irrep, b_irrep, virt_irrep, occ_irrep):
    virt, x, core = lax.axis_index("virt"), lax.axis_index("x"), lax.axis_index("c")
    device = (virt * 4 + x) * 2 + core
    classes = (b_irrep[:, None] ^ occ_irrep[None, :]).reshape(BJ)
    class_row, class_col = classes[None, :], classes[:, None]
    a_rows = lax.dynamic_slice_in_dim(a_irrep, virt * 4, 4, 0)
    i_rows = lax.dynamic_slice_in_dim(occ_irrep, (2 * x + core) * 15, 15, 0)
    row_class = jnp.pad((i_rows[:, None] ^ a_rows[None, :]).reshape(60), (0, 4))[:, None]
    fullest = jnp.max(jnp.sum(classes[:, None] == jnp.arange(8)[None, :], axis=0))

    def one_pass(number):
        first = (number * CAP).astype(jnp.int32)
        place = jnp.stack([device, first]).astype(jnp.int32)
        keep, send = contract(place, a_irrep, b_irrep, virt_irrep, occ_irrep, amplitudes, integrals)
        came = lax.ppermute(send, "c", [(0, 1), (1, 0)])
        arrived = lax.all_to_all(merge(keep, came), ("virt", "x"), 0, 0, tiled=True)
        table = make_table(first[None], class_row, class_col)
        return expand(arrived, table, class_row, row_class)

    passes = lax.div(fullest + (CAP - 1), CAP)
    total = lax.fori_loop(1, passes, lambda n, total: total + one_pass(n), one_pass(jnp.int32(0)))
    return jnp.transpose(total.reshape(15, 4, BJ), (1, 0, 2))


def solution(mesh):
    fine = Mesh(mesh.devices.reshape(16, 4, 2), ("virt", "x", "c"))
    spread = ("virt", "x", "c")
    placed = (P(None, spread, None), P(spread, None, None), P(), P(), P(), P())
    return jax.shard_map(
        on_device, mesh=fine, in_specs=placed, out_specs=P("virt", ("x", "c"), None), check_vma=False
    )
```

time: 528 us -> 89.6 us (0.17)
  waiting for transfers between devices: 432 us -> 28.9 us
  Pallas kernels: 0 us -> 39.4 us
  local copies, waits for them, and re-layouts: 44.1 us -> 6.7 us
  matrix products: 26.7 us -> 0 us
  between operations: 14.1 us -> 0.74 us
    all_to_all x1, waiting for transfers between devices: 278 us -> 24.8 us  [one_pass(): arrived = lax.all_to_all(merge(keep, came), ('virt', 'x'), 0, 0, tiled=True)]
    unnamed x3 -> x0, waiting for transfers between devices: 78 us -> none
    all_gather x1 -> x0, waiting for transfers between devices: 75.7 us -> none  [on_device(): lax.all_gather(integrals, 'virt', axis=0, tiled=True)]
    all_to_all x2 -> x0, local copies, waits for them, and re-layouts: 40.5 us -> none  [on_device(): lax.all_to_all(amplitudes, 'virt', split_axis=0, concat_axis=1, tiled=True)]
    pallas_call x0 -> x4, Pallas kernels: none -> 39.4 us  [the longest x1 29.3 us: contract(): pl.pallas_call(contract_kernel, grid=(1,), in_specs=[sm] * 5 + [any_, any...]
    dot_general x1 -> x0, matrix products: 26.7 us -> none  [contract(): jnp.einsum('aeim,emx->aix', masked, int_block, preferred_element_type=jnp...]
  transfers between devices with their start and end apart: 3 -> 2, of which waited for: 3 -> 2; matrix products, arithmetic and copies ran while one was open for 3% -> 3% of each run, Pallas kernels for 0% -> 3%
where the time goes in v1:
time: 89.6 us; the launch traced here: 89.3 us
  Pallas kernels  39.4 us (44%)
  waiting for transfers between devices  28.9 us (32%)
  starting transfers between devices  11.7 us (13%)
  local copies, waits for them, and re-layouts  6.7 us (7%)
  other arithmetic  1.55 us (2%)
    pallas_call x1, Pallas kernels, contract(): pl.pallas_call(contract_kernel, grid=(1,), in_specs=[sm] * 5 + [any_, any...  29.3 us
    all_to_all x1, waiting for transfers between devices, one_pass(): arrived = lax.all_to_all(merge(keep, came), ('virt', 'x'), 0, 0, tiled=True)  24.8 us
    all_to_all x1, starting transfers between devices, one_pass(): arrived = lax.all_to_all(merge(keep, came), ('virt', 'x'), 0, 0, tiled=True)  11.6 us
    pallas_call x1, Pallas kernels, merge(): pl.pallas_call(merge_kernel, grid=(4,), in_specs=[pl.BlockSpec((1, 15, AW...  5.29 us
    ppermute x1, waiting for transfers between devices, one_pass(): came = lax.ppermute(send, 'c', [(0, 1), (1, 0)])  4.17 us
    unnamed x12, local copies, waits for them, and re-layouts  2.64 us
    pallas_call x1, Pallas kernels, expand(): pl.pallas_call(expand_kernel, grid=(64 // BATCH,), in_specs=[pl.BlockSpec...  2.4 us
    pallas_call x1, Pallas kernels, make_table(): pl.pallas_call(table_kernel, in_specs=[pl.BlockSpec(memory_space=pltpu.SM...  2.4 us
  transfers between devices with their start and end apart: 2, of which 2 were waited for; matrix products, arithmetic and copies ran while one was open for 3% of the time, Pallas kernels for 3%

profile of v1, /device:TPU:0, one launch (start us, length us, event | category | flops | bytes accessed | tf_op | source)
XLA Modules:
  0.0 89.3 jit_solution(7954795058310964441)
XLA Ops:
  0.0 1.2 %pad_bitcast_fusion.2.occ_row = s32[1,128]{1,0:T(1,128)} fusion(s32[120]{0:T(128)} %occ_s.1), kind=kLoop, calls=%fused_computation.11 | loop fusion | bytes 992 | tf_op jit(solution)/shard_map/broadcast_in_dim | solution.py:144
  1.2 0.6 pad_add_fusion.1.place
  1.8 29.3 %contract.2 = (s16[4,15,64,256]{3,2,1,0:T(8,128)(2,1)}, s16[4,15,64,256]{3,2,1,0:T(8,128)(2,1)}) custom-call(s32[2]{0:T(128)} %pad_add_fusion.1.place, s32[64]{0:T(128)} %a_s.1, s32[8]{0:T(128)} %b_s.1, s32[1024]{0:T(1024)} %virt_s.1, s32[120]{0:T(128)} %occ_s.1, bf16[64,8,14400]{2,1,0:T(8,128)(2,1)} %tail.1, bf16[8,120,960]{2,1,0:T(8,128)(2,1)} %ints.1, ...), custom_call_target="tpu_custom_call" | custom-call | tf_op jit(solution)/shard_map/contract/pallas_call | solution.py:145
  31.1 0.1 collective-permute-start.1
  31.2 4.2 %collective-permute-done.1.came = s16[4,15,64,256]{3,2,1,0:T(8,128)(2,1)S(1)} collective-permute-done((s16[4,15,64,256]{3,2,1,0:T(8,128)(2,1)}, s16[4,15,64,256]{3,2,1,0:T(8,128)(2,1)S(1)}, u32[]{:S(2)}, u32[]{:S(2)}) %collective-permute-start.1) | collective-permute-done | bytes 1966112 | tf_op jit(solution)/shard_map/ppermute | solution.py:298
  35.4 1.3 %copy-done.3 = s16[4,15,64,256]{3,2,1,0:T(8,128)(2,1)} copy-done((s16[4,15,64,256]{3,2,1,0:T(8,128)(2,1)}, s16[4,15,64,256]{3,2,1,0:T(8,128)(2,1)S(1)}, u32[]{:S(2)}) %copy-start.3) | copy-done | bytes 1966104
  36.7 5.3 %merge.2 = s16[8,2,4,64,256]{4,3,2,1,0:T(8,128)(2,1)} custom-call(s16[4,15,64,256]{3,2,1,0:T(8,128)(2,1)} %get-tuple-element.77.own, s16[4,15,64,256]{3,2,1,0:T(8,128)(2,1)} %copy-done.3), custom_call_target="tpu_custom_call" | custom-call | tf_op jit(solution)/shard_map/merge/pallas_call | solution.py:197
  42.0 0.0 copy-start.5
  42.0 0.0 copy-start.7
  42.0 11.6 %all-to-all-start.1 = ((s16[64,64,256]{2,1,0:T(8,128)(2,1)}), s16[64,64,256]{2,1,0:T(8,128)(2,1)S(1)}, u32[]{:S(2)}, u32[]{:S(2)}) async-start(s16[64,64,256]{2,1,0:T(8,128)(2,1)} %bitcast.21), calls=%async_computation.1 | async-start | bytes 4194304 | tf_op jit(solution)/shard_map/all_to_all | solution.py:299
  53.7 0.0 copy-done.5
  53.7 0.0 copy-done.6
  53.7 0.1 broadcast_xor_fusion.2
  53.8 0.7 xor.57.class_row
  54.4 1.0 %xor.104.class_col = s32[960,1]{1,0:T(8,128)} reshape(s32[8,120]{1,0:T(8,128)S(1)} %broadcast_xor_fusion.2) | data formatting | bytes 7680 | tf_op jit(solution)/shard_map/xor | solution.py:287
  55.4 0.1 xor.63
  55.5 0.1 dynamic_slice.6
  55.6 0.0 copy-done.7
  55.6 0.1 dynamic_slice.7
  55.6 0.1 broadcast_xor_fusion.1
  55.7 0.1 xor.62
  55.8 0.1 copy.15.row_class
  55.9 0.0 copy-start.4
  55.9 2.4 %table.2 = bf16[256,960]{1,0:T(8,128)(2,1)} custom-call(s32[1]{0:T(128)} %constant.12.clone.1.first, s32[1,960]{1,0:T(1,128)} %xor.57.class_row, s32[960,1]{1,0:T(8,128)} %xor.104.class_col), custom_call_target="tpu_custom_call" | custom-call | tf_op jit(solution)/shard_map/table/pallas_call | solution.py:223
  58.3 0.1 convert_reduce_fusion
  58.4 0.7 reduce_max.9
  59.8 24.8 %all-to-all-done.1.came = s16[64,64,256]{2,1,0:T(8,128)(2,1)S(1)} async-done(((s16[64,64,256]{2,1,0:T(8,128)(2,1)}), s16[64,64,256]{2,1,0:T(8,128)(2,1)S(1)}, u32[]{:S(2)}, u32[]{:S(2)}) %all-to-all-start.1) | async-done | bytes 2097184 | tf_op jit(solution)/shard_map/all_to_all | solution.py:299
  84.5 1.3 %copy-done.2 = s16[64,64,256]{2,1,0:T(8,128)(2,1)} copy-done((s16[64,64,256]{2,1,0:T(8,128)(2,1)}, s16[64,64,256]{2,1,0:T(8,128)(2,1)S(1)}, u32[]{:S(2)}) %copy-start.2) | copy-done | bytes 2097176
  85.9 2.4 %expand.2 = f32[60,960]{1,0:T(8,128)S(1)} custom-call(s16[64,64,256]{2,1,0:T(8,128)(2,1)} %copy-done.2, bf16[256,960]{1,0:T(8,128)(2,1)} %table.2, s32[1,960]{1,0:T(1,128)} %xor.57.class_row, s32[64,1]{1,0:T(8,128)S(1)} %copy.15.row_class), custom_call_target="tpu_custom_call" | custom-call | tf_op jit(solution)/shard_map/expand/pallas_call | solution.py:267
  88.3 0.0 copy-done.4
  88.3 0.2 while.12
  88.5 0.8 reshape.65
  (4 shorter events, 0.0 us)
Async XLA Ops:
  31.1 4.3 %collective-permute-start.1 = (s16[4,15,64,256]{3,2,1,0:T(8,128)(2,1)}, s16[4,15,64,256]{3,2,1,0:T(8,128)(2,1)S(1)}, u32[]{:S(2)}, u32[]{:S(2)}) collective-permute-start(s16[4,15,64,256]{3,2,1,0:T(8,128)(2,1)} %get-tuple-element.78), channel_id=1, source_target_pairs={{0,1},{1,0},{2,3},{3,2},{4,5},{5,4},{6,7},{7,6},{8,9},{9,8},{10,11... | collective-permute-start | bytes 5898248 | tf_op jit(solution)/shard_map/ppermute | solution.py:298
  35.4 1.3 %copy-start.3 = (s16[4,15,64,256]{3,2,1,0:T(8,128)(2,1)}, s16[4,15,64,256]{3,2,1,0:T(8,128)(2,1)S(1)}, u32[]{:S(2)}) copy-start(s16[4,15,64,256]{3,2,1,0:T(8,128)(2,1)S(1)} %collective-permute-done.1.came) | copy-start | bytes 5898244
  42.0 11.7 %copy-start.5 = (s32[8]{0:T(128)S(1)}, s32[8]{0:T(128)}, u32[]{:S(2)}) copy-start(s32[8]{0:T(128)} %b_s.1) | copy-start | bytes 100
  42.0 11.7 %copy-start.6 = (s32[120]{0:T(128)S(1)}, s32[120]{0:T(128)}, u32[]{:S(2)}) copy-start(s32[120]{0:T(128)} %occ_s.1) | copy-start | bytes 1444
  42.0 13.6 %copy-start.7 = (s32[64]{0:T(128)S(1)}, s32[64]{0:T(128)}, u32[]{:S(2)}) copy-start(s32[64]{0:T(128)} %a_s.1) | copy-start | bytes 772
  42.0 42.5 %all-to-all-start.1 = ((s16[64,64,256]{2,1,0:T(8,128)(2,1)}), s16[64,64,256]{2,1,0:T(8,128)(2,1)S(1)}, u32[]{:S(2)}, u32[]{:S(2)}) async-start(s16[64,64,256]{2,1,0:T(8,128)(2,1)} %bitcast.21), calls=%async_computation.1 | async-start | bytes 4194304 | tf_op jit(solution)/shard_map/all_to_all | solution.py:299
  55.9 32.4 %copy-start.4 = (s32[1024]{0:T(1024)S(1)}, s32[1024]{0:T(1024)}, u32[]{:S(2)}) copy-start(s32[1024]{0:T(1024)} %virt_s.1) | copy-start | bytes 12292
  84.5 1.3 %copy-start.2 = (s16[64,64,256]{2,1,0:T(8,128)(2,1)}, s16[64,64,256]{2,1,0:T(8,128)(2,1)S(1)}, u32[]{:S(2)}) copy-start(s16[64,64,256]{2,1,0:T(8,128)(2,1)S(1)} %all-to-all-done.1.came) | copy-start | bytes 6291460

commit v2 on v0

v2 whole, which is shorter than its diff:
```python
import functools

import jax
import jax.numpy as jnp
from jax import lax
from jax.experimental import pallas as pl
from jax.experimental.pallas import tpu as pltpu
from jax.sharding import Mesh, PartitionSpec as P

O = 120
BJ = 960
AW = 64
CAP = 256
LANES = 256
MIB = 1024 * 1024


GROUP = 5
ROWS = 15 * AW
CODED = ROWS + 16


def unit_codes(unit):
    unit = jnp.maximum(unit, 1e-30)
    power = jnp.floor(jnp.log2(unit)) - 13.0
    return power, jnp.floor(unit * jnp.exp2(-power)) + 1.0


def unit_of(power, mantissa):
    return mantissa * jnp.exp2(power)


def pack_rows(first, e_labels, b_s, ints, occ_line, weights):
    diagonal = lax.broadcasted_iota(jnp.int32, (128, 128), 0) == lax.broadcasted_iota(jnp.int32, (128, 128), 1)
    occ_col = jnp.sum(jnp.where(diagonal, jnp.broadcast_to(occ_line, (128, 128)), 0), axis=1, keepdims=True)
    lane = lax.broadcasted_iota(jnp.int32, (128, BJ), 1)
    row = lax.broadcasted_iota(jnp.int32, (128, BJ), 0)
    column = lax.broadcasted_iota(jnp.int32, (1, BJ), 1)
    hit = jnp.zeros((128, BJ), jnp.bool_)
    b_row = jnp.zeros((1, BJ), jnp.int32)
    for b in range(8):
        hit = hit | (lane - b * O == row)
        b_row = jnp.where(column >= b * O, b_s[b], b_row)
    hit = hit & (row < O)
    class_row = jnp.sum(jnp.where(hit, occ_col, 0), axis=0, keepdims=True) ^ b_row
    occ_col = occ_col[:O]
    picks = []
    for part in range(8):
        mine = lax.broadcasted_iota(jnp.int32, (O, BJ), 0) + part * O
        other = lax.broadcasted_iota(jnp.int32, (O, BJ), 1)
        same = ((occ_col ^ b_s[part]) == class_row) & (other < mine)
        rank = jnp.sum(jnp.where(same, 1.0, 0.0), axis=1, keepdims=True) - first.astype(jnp.float32)
        slot = lax.broadcasted_iota(jnp.int32, (O, LANES), 1).astype(jnp.float32)
        picks.append(jnp.where(rank == slot, 1.0, 0.0))
    pick = jnp.concatenate(picks, axis=0).astype(jnp.bfloat16)
    for e in range(8):
        kept = jnp.where((occ_col ^ e_labels[e]) == class_row, ints[e].astype(jnp.float32), 0.0)
        packed = jnp.dot(kept.astype(jnp.bfloat16), pick, preferred_element_type=jnp.float32)
        whole = jnp.concatenate([packed, jnp.zeros((128 - O, LANES), jnp.float32)], axis=0)
        weights[e * 128 : (e + 1) * 128, :] = whole.astype(jnp.bfloat16)


def contract_kernel(
    keeps, first, a_s, b_s, virt_s, occ_s, amp, edge, last, occ_in, source, *rest
):
    if keeps:
        out, buf, labels, stage, left, codes, lines, in_sems, out_sems = rest
        weights = source
    else:
        out, weights, buf, labels, stage, left, codes, lines, in_sems, out_sems, ints, ints_sem = rest
    core = lax.axis_index("c")
    device = (lax.axis_index("virt") * 4 + lax.axis_index("x")) * 2 + core
    half = core if keeps else 1 - core

    def read(x):
        start = pl.multiple_of(128 * (28 * x + 14 * half), 128)
        size = 1792 if x == 3 else 1920
        return pltpu.make_async_copy(
            amp.at[:, :, pl.ds(start, size)], buf.at[x, :, :, pl.ds(0, size)], in_sems.at[x]
        )

    reads = [read(x) for x in range(4)]
    e_labels = [virt_s[device * 8 + e] for e in range(8)]
    lines[...] = jnp.zeros_like(lines)
    lines[0:1, :O] = occ_in[...].astype(jnp.float32)
    occ_line = lines[0:1, :128].astype(jnp.int32)
    if not keeps:
        fetch = pltpu.make_async_copy(source, ints, ints_sem)
        fetch.start()
    reads[0].start()
    reads[1].start()
    row = lax.broadcasted_iota(jnp.int32, (8, 128), 0)
    e_label = jnp.zeros((8, 128), jnp.int32)
    for e in range(8):
        e_label = jnp.where(row == e, e_labels[e], e_label)
    for a in range(AW):
        labels[a] = e_label ^ a_s[a]
    buf[3, :, :, 1792:] = jnp.where(half == 0, edge[...], last[...])
    if not keeps:
        fetch.wait()
        pack_rows(first[0], e_labels, b_s, ints, occ_line, weights)
    lane = lax.broadcasted_iota(jnp.int32, (AW, 8, 128), 2)
    lanes = lax.broadcasted_iota(jnp.int32, (8, 128), 1)
    occ_rows = jnp.where(lanes < O, jnp.broadcast_to(occ_line, (8, 128)), 64)
    def write(x):
        return pltpu.make_async_copy(codes.at[x], out.at[x], out_sems.at[x])

    def block(x, carry):
        for n in range(4):

            @pl.when(x == n)
            def _():
                reads[n].wait()
                if n < 2:
                    reads[n + 2].start()

        for number in range(15 // GROUP):
            for u in range(GROUP):
                inner = number * GROUP + u
                flat = 16 * x + 8 * half + O * inner
                tile = lax.div(flat, 128)
                offset = flat - 128 * tile
                now = buf[x, :, :, pl.ds(pl.multiple_of(tile * 128, 128), 128)].astype(jnp.float32)
                after = buf[x, :, :, pl.ds(pl.multiple_of(tile * 128 + 128, 128), 128)].astype(jnp.float32)
                row = pltpu.roll(jnp.where(lane >= offset, now, after), lax.rem(128 - offset, 128), axis=2)
                pair = occ_rows ^ occ_s[30 * x + 15 * half + inner]
                row = jnp.where(labels[...] == pair[None], row, 0.0)
                for a in range(AW):
                    stage[number, pl.ds(u * 520 + a, 8, stride=65), :] = row[a]
                for e in range(8):
                    rows = stage[number, pl.ds(u * 520 + 65 * e, AW), :]
                    left[number, u * AW : (u + 1) * AW, e * 128 : (e + 1) * 128] = rows.astype(jnp.bfloat16)
            total = jnp.dot(left[number], weights[...], preferred_element_type=jnp.float32)
            largest = jnp.max(jnp.abs(total), axis=0, keepdims=True)
            power, mantissa = unit_codes(largest * (1.0001 / 32767.0))
            lines[2 * number : 2 * number + 1, :] = power
            lines[2 * number + 1 : 2 * number + 2, :] = mantissa
            coded = jnp.round(total * (1.0 / unit_of(power, mantissa)))
            codes[x, number * GROUP * AW : (number + 1) * GROUP * AW, :] = coded.astype(jnp.int16)
        codes[x, ROWS:, :] = jnp.concatenate([lines[...], lines[...]], axis=0).astype(jnp.int16)
        write(x).start()
        return carry

    lax.fori_loop(0, 4, block, 0)
    for x in range(4):
        write(x).wait()


def contract(keeps, first, a, b, virt, occ, amp, source):
    any_, sm, vm = (pl.BlockSpec(memory_space=space) for space in (pl.ANY, pltpu.SMEM, pltpu.VMEM))
    coded = jax.ShapeDtypeStruct((4, CODED, LANES), jnp.int16)
    packed = jax.ShapeDtypeStruct((1024, LANES), jnp.bfloat16)
    scratch = [
        pltpu.VMEM((4, AW, 8, 15 * 128), jnp.bfloat16),
        pltpu.VMEM((AW, 8, 128), jnp.int32),
        pltpu.VMEM((15 // GROUP, GROUP * 520, 128), jnp.float32),
        pltpu.VMEM((15 // GROUP, GROUP * AW, 1024), jnp.bfloat16),
        pltpu.VMEM((4, CODED, LANES), jnp.int16),
        pltpu.VMEM((8, LANES), jnp.float32),
        pltpu.SemaphoreType.DMA((4,)),
        pltpu.SemaphoreType.DMA((4,)),
    ]
    if not keeps:
        scratch += [pltpu.VMEM((8, O, BJ), jnp.bfloat16), pltpu.SemaphoreType.DMA]
    return pl.pallas_call(
        functools.partial(contract_kernel, keeps),
        grid=(1,),
        in_specs=[sm] * 5
        + [
            any_,
            pl.BlockSpec((AW, 8, 128), lambda s: (0, 0, 98)),
            pl.BlockSpec((AW, 8, 128), lambda s: (0, 0, 112)),
            vm,
            vm if keeps else any_,
        ],
        out_specs=any_ if keeps else [any_, vm],
        scratch_shapes=scratch,
        out_shape=coded if keeps else [coded, packed],
        cost_estimate=pl.CostEstimate(flops=8 * 10**9, bytes_accessed=12 * 10**6, transcendentals=0),
        compiler_params=pltpu.CompilerParams(vmem_limit_bytes=44 * MIB),
        name="contract_keep" if keeps else "contract_send",
    )(first, a, b, virt, occ, amp, amp, amp, occ[None], source)


def merge_kernel(own, came, out):
    own_lines = own[0, ROWS:, :].astype(jnp.float32)
    came_lines = came[0, ROWS:, :].astype(jnp.float32)
    units = []
    for g in range(3):
        units.append([unit_of(l[2 * g : 2 * g + 1], l[2 * g + 1 : 2 * g + 2]) for l in (own_lines, came_lines)])
    power, mantissa = unit_codes(1.0001 * jnp.maximum(jnp.maximum(sum(units[0]), sum(units[1])), sum(units[2])))
    inverse = 1.0 / unit_of(power, mantissa)
    codes = jnp.concatenate([power, mantissa, power, mantissa], axis=0)
    codes = jnp.broadcast_to(codes[None], (8, 4, LANES))
    for quad in range(4):
        sums = []
        for inner in range(4 * quad, min(4 * quad + 4, 15)):
            rows = slice(inner * AW, (inner + 1) * AW)
            one, two = (unit * inverse for unit in units[inner // GROUP])
            total = jnp.round(own[0, rows, :].astype(jnp.float32) * one + came[0, rows, :].astype(jnp.float32) * two)
            sums.append(total.reshape(8, 8, LANES))
        for half in range(2):
            rows = [s[:, 4 * half : 4 * half + 4] for s in sums] + ([codes] if quad == 3 else [])
            out[:, half, 0, 16 * quad : 16 * quad + 16, :] = jnp.concatenate(rows, axis=1).astype(jnp.int16)


def merge(own, came):
    out = pl.pallas_call(
        merge_kernel,
        grid=(4,),
        in_specs=[pl.BlockSpec((1, CODED, LANES), lambda x: (x, 0, 0))] * 2,
        out_specs=pl.BlockSpec((8, 2, 1, 64, LANES), lambda x: (0, 0, x, 0, 0)),
        out_shape=jax.ShapeDtypeStruct((8, 2, 4, 64, LANES), jnp.int16),
        compiler_params=pltpu.CompilerParams(vmem_limit_bytes=14 * MIB),
        name="merge",
    )(own, came)
    return out.reshape(64, 64, LANES)


def table_kernel(first, class_row, class_col, table):
    shape = (O, BJ)
    rank = jnp.zeros((1, BJ), jnp.float32)
    for part in range(8):
        before = lax.broadcasted_iota(jnp.int32, shape, 0) + part * O < lax.broadcasted_iota(jnp.int32, shape, 1)
        same = (class_col[part * O : (part + 1) * O, :] == class_row[...]) & before
        rank = rank + jnp.sum(jnp.where(same, 1.0, 0.0), axis=0, keepdims=True)
    slot = lax.broadcasted_iota(jnp.int32, (LANES, BJ), 0).astype(jnp.float32)
    chosen = rank - first[0].astype(jnp.float32) == slot
    table[...] = jnp.where(chosen, 1.0, 0.0).astype(jnp.bfloat16)


def make_table(first, class_row, class_col):
    vm = pl.BlockSpec(memory_space=pltpu.VMEM)
    return pl.pallas_call(
        table_kernel,
        in_specs=[pl.BlockSpec(memory_space=pltpu.SMEM), vm, vm],
        out_specs=vm,
        out_shape=jax.ShapeDtypeStruct((LANES, BJ), jnp.bfloat16),
        compiler_params=pltpu.CompilerParams(vmem_limit_bytes=14 * MIB),
        name="table",
    )(first, class_row, class_col)


BATCH = 32


def expand_kernel(came, table, class_row, row_class, out, total):
    step = pl.program_id(0)
    part = jnp.zeros((64, LANES), jnp.float32)
    for n in range(BATCH):
        values = came[n].astype(jnp.float32)
        part = part + values * unit_of(values[60:61], values[61:62])

    @pl.when(step == 0)
    def _():
        total[...] = part

    @pl.when(step > 0)
    def _():
        total[...] = total[...] + part

    @pl.when(step == pl.num_programs(0) - 1)
    def _():
        value = total[...]
        high = value.astype(jnp.bfloat16)
        rest = value - high.astype(jnp.float32)
        middle = rest.astype(jnp.bfloat16)
        low = (rest - middle.astype(jnp.float32)).astype(jnp.bfloat16)
        parts = jnp.concatenate([high, middle, low], axis=0)
        spread = jnp.dot(parts, table[...], preferred_element_type=jnp.float32)
        spread = spread[:64] + (spread[64:128] + spread[128:])
        out[...] = jnp.where(row_class[...] == class_row[...], spread, 0.0)[:60]


def expand(came, table, class_row, row_class):
    whole = lambda *shape: pl.BlockSpec(shape, lambda n: (0,) * len(shape))
    return pl.pallas_call(
        expand_kernel,
        grid=(64 // BATCH,),
        in_specs=[
            pl.BlockSpec((BATCH, 64, LANES), lambda n: (n, 0, 0)),
            whole(LANES, BJ),
            whole(1, BJ),
            whole(64, 1),
        ],
        out_specs=whole(60, BJ),
        out_shape=jax.ShapeDtypeStruct((60, BJ), jnp.float32),
        scratch_shapes=[pltpu.VMEM((64, LANES), jnp.float32)],
        compiler_params=pltpu.CompilerParams(vmem_limit_bytes=14 * MIB),
        name="expand",
    )(came, table, class_row, row_class)


def on_device(amplitudes, integrals, a_irrep, b_irrep, virt_irrep, occ_irrep):
    virt, x, core = lax.axis_index("virt"), lax.axis_index("x"), lax.axis_index("c")
    classes = (b_irrep[:, None] ^ occ_irrep[None, :]).reshape(BJ)
    class_row, class_col = classes[None, :], classes[:, None]
    a_rows = lax.dynamic_slice_in_dim(a_irrep, virt * 4, 4, 0)
    i_rows = lax.dynamic_slice_in_dim(occ_irrep, (2 * x + core) * 15, 15, 0)
    row_class = jnp.pad((i_rows[:, None] ^ a_rows[None, :]).reshape(60), (0, 4))[:, None]
    fullest = jnp.max(jnp.sum(classes[:, None] == jnp.arange(8)[None, :], axis=0))

    def one_pass(number):
        first = (number * CAP).astype(jnp.int32)[None]
        labels = a_irrep, b_irrep, virt_irrep, occ_irrep
        send, weights = contract(False, first, *labels, amplitudes, integrals)
        came = lax.ppermute(send, "c", [(0, 1), (1, 0)])
        keep = contract(True, first, *labels, amplitudes, weights)
        arrived = lax.all_to_all(merge(keep, came), ("virt", "x"), 0, 0, tiled=True)
        table = make_table(first, class_row, class_col)
        return expand(arrived, table, class_row, row_class)

    passes = lax.div(fullest + (CAP - 1), CAP)
    total = lax.fori_loop(1, passes, lambda n, total: total + one_pass(n), one_pass(jnp.int32(0)))
    return jnp.transpose(total.reshape(15, 4, BJ), (1, 0, 2))


def solution(mesh):
    fine = Mesh(mesh.devices.reshape(16, 4, 2), ("virt", "x", "c"))
    spread = ("virt", "x", "c")
    placed = (P(None, spread, None), P(spread, None, None), P(), P(), P(), P())
    return jax.shard_map(
        on_device, mesh=fine, in_specs=placed, out_specs=P("virt", ("x", "c"), None), check_vma=False
    )
```

time: 528 us -> 74.7 us (0.14)
  waiting for transfers between devices: 432 us -> 28.6 us
  local copies, waits for them, and re-layouts: 44.1 us -> 1.47 us
  Pallas kernels: 0 us -> 30.9 us
  matrix products: 26.7 us -> 0 us
  between operations: 14.1 us -> 0.79 us
    all_to_all x1, waiting for transfers between devices: 278 us -> 28.6 us  [one_pass(): arrived = lax.all_to_all(merge(keep, came), ('virt', 'x'), 0, 0, tiled=True)]
    unnamed x3 -> x0, waiting for transfers between devices: 78 us -> none
    all_gather x1 -> x0, waiting for transfers between devices: 75.7 us -> none  [on_device(): lax.all_gather(integrals, 'virt', axis=0, tiled=True)]
    all_to_all x2 -> x0, local copies, waits for them, and re-layouts: 40.5 us -> none  [on_device(): lax.all_to_all(amplitudes, 'virt', split_axis=0, concat_axis=1, tiled=True)]
    pallas_call x0 -> x5, Pallas kernels: none -> 30.9 us  [the longest x2 26.1 us: contract(): pl.pallas_call(functools.partial(contract_kernel, keeps), grid=(1,), in_s...]
    dot_general x1 -> x0, matrix products: 26.7 us -> none  [contract(): jnp.einsum('aeim,emx->aix', masked, int_block, preferred_element_type=jnp...]
  transfers between devices with their start and end apart: 3 -> 2, of which waited for: 3 -> 1; matrix products, arithmetic and copies ran while one was open for 3% -> 2% of each run, Pallas kernels for 0% -> 17%
where the time goes in v2:
time: 74.7 us; the launch traced here: 74.4 us
  Pallas kernels  30.9 us (41%)
  waiting for transfers between devices  28.6 us (38%)
  starting transfers between devices  11.6 us (16%)
  local copies, waits for them, and re-layouts  1.47 us (2%)
  other arithmetic  0.91 us (1%)
  between operations  0.79 us (1%)
    all_to_all x1, waiting for transfers between devices, one_pass(): arrived = lax.all_to_all(merge(keep, came), ('virt', 'x'), 0, 0, tiled=True)  28.6 us
    pallas_call x2, Pallas kernels, contract(): pl.pallas_call(functools.partial(contract_kernel, keeps), grid=(1,), in_s...  26.1 us
    all_to_all x1, starting transfers between devices, one_pass(): arrived = lax.all_to_all(merge(keep, came), ('virt', 'x'), 0, 0, tiled=True)  11.5 us
    pallas_call x1, Pallas kernels, merge(): pl.pallas_call(merge_kernel, grid=(4,), in_specs=[pl.BlockSpec((1, CODED,...  3.24 us
  transfers between devices with their start and end apart: 2, of which 1 were waited for; matrix products, arithmetic and copies ran while one was open for 2% of the time, Pallas kernels for 17%

profile of v2, /device:TPU:0, one launch (start us, length us, event | category | flops | bytes accessed | tf_op | source)
XLA Modules:
  0.0 74.4 jit_solution(5784062061702513165)
XLA Ops:
  0.0 0.0 copy-start
  0.0 0.0 copy-start.1
  0.0 0.0 copy-start.2
  0.0 0.0 copy-start.3
  0.0 14.2 %contract_send.2 = (s16[4,976,256]{2,1,0:T(8,128)(2,1)S(1)}, bf16[1024,256]{1,0:T(8,128)(2,1)S(1)}) custom-call(s32[1]{0:T(128)} %constant.8.clone.1.first, s32[64]{0:T(128)} %a_s.3, s32[8]{0:T(128)} %b_s.3, s32[1024]{0:T(1024)} %virt_s.3, s32[120]{0:T(128)} %occ_s.3, bf16[64,8,14400]{2,1,0:T(8,128)(2,1)} %last.3, bf16[64,8,14400]{2,1,0:T(8,128)(2,1)} %last.3, ...), custom_call_target="tpu_custom_call" | custom-call | flops 8000000000 | bytes 12000000 | tf_op jit(solution)/shard_map/contract_send/pallas_call | solution.py:165
  14.2 0.1 collective-permute-start.1
  14.3 0.0 copy-done
  14.3 0.0 copy-done.1
  14.4 0.0 copy-done.2
  14.4 0.0 copy-done.3
  14.4 11.9 %contract_keep.2.own = s16[4,976,256]{2,1,0:T(8,128)(2,1)S(1)} custom-call(s32[1]{0:T(128)} %constant.8.clone.1.first, s32[64]{0:T(128)S(1)} %copy-done.3, s32[8]{0:T(128)S(1)} %copy-done.2, s32[1024]{0:T(1024)S(1)} %copy-done, s32[120]{0:T(128)S(1)} %copy-done.1, bf16[64,8,14400]{2,1,0:T(8,128)(2,1)} %last.3, bf16[64,8,14400]{2,1,0:T(8,128)(2,1)} %last.3, ...), custom_call_target="tpu_custom_call" | custom-call | flops 8000000000 | bytes 12000000 | tf_op jit(solution)/shard_map/contract_keep/pallas_call | solution.py:165
  26.3 0.0 collective-permute-done.1.came
  26.3 3.2 %merge.2 = s16[8,2,4,64,256]{4,3,2,1,0:T(8,128)(2,1)} custom-call(s16[4,976,256]{2,1,0:T(8,128)(2,1)S(1)} %contract_keep.2.own, s16[4,976,256]{2,1,0:T(8,128)(2,1)S(1)} %collective-permute-done.1.came), custom_call_target="tpu_custom_call" | custom-call | tf_op jit(solution)/shard_map/merge/pallas_call | solution.py:208
  29.6 11.5 %all-to-all-start.1 = ((s16[64,64,256]{2,1,0:T(8,128)(2,1)}), s16[64,64,256]{2,1,0:T(8,128)(2,1)S(1)}, u32[]{:S(2)}, u32[]{:S(2)}) async-start(s16[64,64,256]{2,1,0:T(8,128)(2,1)} %bitcast.1), calls=%async_computation.1 | async-start | bytes 4194304 | tf_op jit(solution)/shard_map/all_to_all | solution.py:309
  41.1 0.1 broadcast_xor_fusion.2
  41.1 0.1 xor.57.class_row
  41.2 0.2 xor.104.class_col
  41.4 0.1 xor.63
  41.5 0.1 convert_reduce_fusion
  41.6 0.6 reduce_max.9
  42.9 0.1 dynamic_slice.6
  43.0 0.1 dynamic_slice.7
  43.1 0.1 broadcast_xor_fusion.1
  43.2 0.1 xor.62
  43.3 0.1 copy.15.row_class
  43.4 0.5 table.2
  43.9 28.6 %all-to-all-done.1.came = s16[64,64,256]{2,1,0:T(8,128)(2,1)S(1)} async-done(((s16[64,64,256]{2,1,0:T(8,128)(2,1)}), s16[64,64,256]{2,1,0:T(8,128)(2,1)S(1)}, u32[]{:S(2)}, u32[]{:S(2)}) %all-to-all-start.1) | async-done | bytes 2097184 | tf_op jit(solution)/shard_map/all_to_all | solution.py:309
  72.5 1.0 %expand.2 = f32[60,960]{1,0:T(8,128)S(1)} custom-call(s16[64,64,256]{2,1,0:T(8,128)(2,1)S(1)} %all-to-all-done.1.came, bf16[256,960]{1,0:T(8,128)(2,1)S(1)} %table.2, s32[1,960]{1,0:T(1,128)S(1)} %xor.57.class_row, s32[64,1]{1,0:T(8,128)S(1)} %copy.15.row_class), custom_call_target="tpu_custom_call" | custom-call | tf_op jit(solution)/shard_map/expand/pallas_call | solution.py:277
  73.5 0.2 while.12
  73.7 0.8 %reshape.65 = f32[15,4,960]{2,1,0:T(4,128)} reshape(f32[60,960]{1,0:T(8,128)S(1)} %get-tuple-element.74) | data formatting | bytes 460800 | tf_op jit(solution)/shard_map/reshape | solution.py:315
  (1 shorter events, 0.0 us)
Async XLA Ops:
  0.0 14.3 %copy-start = (s32[1024]{0:T(1024)S(1)}, s32[1024]{0:T(1024)}, u32[]{:S(2)}) copy-start(s32[1024]{0:T(1024)} %virt_s.3) | copy-start | bytes 12292
  0.0 14.3 %copy-start.1 = (s32[120]{0:T(128)S(1)}, s32[120]{0:T(128)}, u32[]{:S(2)}) copy-start(s32[120]{0:T(128)} %occ_s.3) | copy-start | bytes 1444
  0.0 14.4 %copy-start.2 = (s32[8]{0:T(128)S(1)}, s32[8]{0:T(128)}, u32[]{:S(2)}) copy-start(s32[8]{0:T(128)} %b_s.3) | copy-start | bytes 100
  0.0 14.4 %copy-start.3 = (s32[64]{0:T(128)S(1)}, s32[64]{0:T(128)}, u32[]{:S(2)}) copy-start(s32[64]{0:T(128)} %a_s.3) | copy-start | bytes 772
  14.2 12.1 %collective-permute-start.1 = (s16[4,976,256]{2,1,0:T(8,128)(2,1)S(1)}, s16[4,976,256]{2,1,0:T(8,128)(2,1)S(1)}, u32[]{:S(2)}, u32[]{:S(2)}) collective-permute-start(s16[4,976,256]{2,1,0:T(8,128)(2,1)S(1)} %get-tuple-element.73), channel_id=1, source_target_pairs={{0,1},{1,0},{2,3},{3,2},{4,5},{5,4},{6,7},{7,6},{8,9},{9,8},{10,11... | collective-permute-start | bytes 5996552 | tf_op jit(solution)/shard_map/ppermute | solution.py:307
  29.6 42.9 %all-to-all-start.1 = ((s16[64,64,256]{2,1,0:T(8,128)(2,1)}), s16[64,64,256]{2,1,0:T(8,128)(2,1)S(1)}, u32[]{:S(2)}, u32[]{:S(2)}) async-start(s16[64,64,256]{2,1,0:T(8,128)(2,1)} %bitcast.1), calls=%async_computation.1 | async-start | bytes 4194304 | tf_op jit(solution)/shard_map/all_to_all | solution.py:309

commit v3 on v2

--- a/solution.py
+++ b/solution.py
@@ -30,7 +30,7 @@
     return mantissa * jnp.exp2(power)
 
 
-def pack_rows(first, e_labels, b_s, ints, occ_line, weights):
+def pack_rows(first, e_labels, b_s, ints, occ_line, weights, fullest):
     diagonal = lax.broadcasted_iota(jnp.int32, (128, 128), 0) == lax.broadcasted_iota(jnp.int32, (128, 128), 1)
     occ_col = jnp.sum(jnp.where(diagonal, jnp.broadcast_to(occ_line, (128, 128)), 0), axis=1, keepdims=True)
     lane = lax.broadcasted_iota(jnp.int32, (128, BJ), 1)
@@ -45,13 +45,16 @@
     class_row = jnp.sum(jnp.where(hit, occ_col, 0), axis=0, keepdims=True) ^ b_row
     occ_col = occ_col[:O]
     picks = []
+    highest = jnp.zeros((O, 1), jnp.float32)
     for part in range(8):
         mine = lax.broadcasted_iota(jnp.int32, (O, BJ), 0) + part * O
         other = lax.broadcasted_iota(jnp.int32, (O, BJ), 1)
         same = ((occ_col ^ b_s[part]) == class_row) & (other < mine)
-        rank = jnp.sum(jnp.where(same, 1.0, 0.0), axis=1, keepdims=True) - first.astype(jnp.float32)
+        rank = jnp.sum(jnp.where(same, 1.0, 0.0), axis=1, keepdims=True)
+        highest = jnp.maximum(highest, rank)
         slot = lax.broadcasted_iota(jnp.int32, (O, LANES), 1).astype(jnp.float32)
-        picks.append(jnp.where(rank == slot, 1.0, 0.0))
+        picks.append(jnp.where(rank - first.astype(jnp.float32) == slot, 1.0, 0.0))
+    fullest[0] = jnp.max(highest).astype(jnp.int32) + 1
     pick = jnp.concatenate(picks, axis=0).astype(jnp.bfloat16)
     for e in range(8):
         kept = jnp.where((occ_col ^ e_labels[e]) == class_row, ints[e].astype(jnp.float32), 0.0)
@@ -67,7 +70,7 @@
         out, buf, labels, stage, left, codes, lines, in_sems, out_sems = rest
         weights = source
     else:
-        out, weights, buf, labels, stage, left, codes, lines, in_sems, out_sems, ints, ints_sem = rest
+        out, weights, fullest, buf, labels, stage, left, codes, lines, in_sems, out_sems, ints, ints_sem = rest
     core = lax.axis_index("c")
     device = (lax.axis_index("virt") * 4 + lax.axis_index("x")) * 2 + core
     half = core if keeps else 1 - core
@@ -98,7 +101,7 @@
     buf[3, :, :, 1792:] = jnp.where(half == 0, edge[...], last[...])
     if not keeps:
         fetch.wait()
-        pack_rows(first[0], e_labels, b_s, ints, occ_line, weights)
+        pack_rows(first[0], e_labels, b_s, ints, occ_line, weights, fullest)
     lane = lax.broadcasted_iota(jnp.int32, (AW, 8, 128), 2)
     lanes = lax.broadcasted_iota(jnp.int32, (8, 128), 1)
     occ_rows = jnp.where(lanes < O, jnp.broadcast_to(occ_line, (8, 128)), 64)
@@ -173,16 +176,16 @@
             vm,
             vm if keeps else any_,
         ],
-        out_specs=any_ if keeps else [any_, vm],
+        out_specs=any_ if keeps else [any_, vm, sm],
         scratch_shapes=scratch,
-        out_shape=coded if keeps else [coded, packed],
+        out_shape=coded if keeps else [coded, packed, jax.ShapeDtypeStruct((1,), jnp.int32)],
         cost_estimate=pl.CostEstimate(flops=8 * 10**9, bytes_accessed=12 * 10**6, transcendentals=0),
         compiler_params=pltpu.CompilerParams(vmem_limit_bytes=44 * MIB),
         name="contract_keep" if keeps else "contract_send",
     )(first, a, b, virt, occ, amp, amp, amp, occ[None], source)
 
 
-def merge_kernel(own, came, out):
+def merge_kernel(own, came, out, more):
     own_lines = own[0, ROWS:, :].astype(jnp.float32)
     came_lines = came[0, ROWS:, :].astype(jnp.float32)
     units = []
@@ -192,6 +195,7 @@
     inverse = 1.0 / unit_of(power, mantissa)
     codes = jnp.concatenate([power, mantissa, power, mantissa], axis=0)
     codes = jnp.broadcast_to(codes[None], (8, 4, LANES))
+    wide_part = [[], []]
     for quad in range(4):
         sums = []
         for inner in range(4 * quad, min(4 * quad + 4, 15)):
@@ -201,20 +205,33 @@
             sums.append(total.reshape(8, 8, LANES))
         for half in range(2):
             rows = [s[:, 4 * half : 4 * half + 4] for s in sums] + ([codes] if quad == 3 else [])
-            out[:, half, 0, 16 * quad : 16 * quad + 16, :] = jnp.concatenate(rows, axis=1).astype(jnp.int16)
+            rows = jnp.concatenate(rows, axis=1)
+            out[:, half, 0, 16 * quad : 16 * quad + 16, :] = rows[:, :, :128].astype(jnp.int16)
+            wide_part[half].append(rows[:, :, 128:])
+    lane = lax.broadcasted_iota(jnp.int32, (8, 16, 128), 2)
+    for half in range(2):
+        for quad in range(2):
+            lower, upper = wide_part[half][quad], wide_part[half][quad + 2]
+            turned = pltpu.roll(upper.reshape(128, 128), 64, axis=1).reshape(8, 16, 128)
+            rows = jnp.where(lane < 64, lower, turned)
+            out[:, half, 0, 64 + 16 * quad : 80 + 16 * quad, :] = rows.astype(jnp.int16)
+            turned = pltpu.roll(lower.reshape(128, 128), 64, axis=1).reshape(8, 16, 128)
+            rows = jnp.where(lane < 64, turned, upper)
+            more[:, half, 0, 16 * quad : 16 * quad + 16, :] = rows.astype(jnp.int16)
 
 
 def merge(own, came):
-    out = pl.pallas_call(
+    shape = lambda rows: (8, 2, 4, rows, 128)
+    out, more = pl.pallas_call(
         merge_kernel,
         grid=(4,),
         in_specs=[pl.BlockSpec((1, CODED, LANES), lambda x: (x, 0, 0))] * 2,
-        out_specs=pl.BlockSpec((8, 2, 1, 64, LANES), lambda x: (0, 0, x, 0, 0)),
-        out_shape=jax.ShapeDtypeStruct((8, 2, 4, 64, LANES), jnp.int16),
+        out_specs=[pl.BlockSpec((8, 2, 1, rows, 128), lambda x: (0, 0, x, 0, 0)) for rows in (96, 32)],
+        out_shape=[jax.ShapeDtypeStruct(shape(rows), jnp.int16) for rows in (96, 32)],
         compiler_params=pltpu.CompilerParams(vmem_limit_bytes=14 * MIB),
         name="merge",
     )(own, came)
-    return out.reshape(64, 64, LANES)
+    return out.reshape(64, 96, 128), more.reshape(64, 32, 128)
 
 
 def table_kernel(first, class_row, class_col, table):
@@ -244,12 +261,21 @@
 BATCH = 32
 
 
-def expand_kernel(came, table, class_row, row_class, out, total):
+def expand_kernel(narrow, came, table, class_row, row_class, out, total):
     step = pl.program_id(0)
-    part = jnp.zeros((64, LANES), jnp.float32)
+    part = jnp.zeros(came.shape[1:], jnp.float32)
+    lane = lax.broadcasted_iota(jnp.int32, (1, 128), 1)
     for n in range(BATCH):
         values = came[n].astype(jnp.float32)
-        part = part + values * unit_of(values[60:61], values[61:62])
+        parts = [values[:64] * unit_of(values[60:61], values[61:62])]
+        unit = unit_of(values[92:93], values[93:94])
+        turned = pltpu.roll(unit, 64, axis=1)
+        parts.append(values[64:96] * jnp.where(lane < 64, turned, unit))
+        if not narrow:
+            unit = unit_of(values[124:125], values[125:126])
+            turned = pltpu.roll(unit, 64, axis=1)
+            parts.append(values[96:] * jnp.where(lane < 64, turned, unit))
+        part = part + jnp.concatenate(parts, axis=0)
 
     @pl.when(step == 0)
     def _():
@@ -262,6 +288,11 @@
     @pl.when(step == pl.num_programs(0) - 1)
     def _():
         value = total[...]
+        third = jnp.concatenate([value[64:96], pltpu.roll(value[64:96], 64, axis=1)], axis=0)
+        last = 0.0
+        if not narrow:
+            last = jnp.concatenate([pltpu.roll(value[96:], 64, axis=1), value[96:]], axis=0)
+        value = jnp.concatenate([value[:64], jnp.where(lane < 64, third, last)], axis=1)
         high = value.astype(jnp.bfloat16)
         rest = value - high.astype(jnp.float32)
         middle = rest.astype(jnp.bfloat16)
@@ -272,46 +303,60 @@
         out[...] = jnp.where(row_class[...] == class_row[...], spread, 0.0)[:60]
 
 
-def expand(came, table, class_row, row_class):
+def expand(narrow, came, table, class_row, row_class):
     whole = lambda *shape: pl.BlockSpec(shape, lambda n: (0,) * len(shape))
+    sent = came.shape[1:]
     return pl.pallas_call(
-        expand_kernel,
+        functools.partial(expand_kernel, narrow),
         grid=(64 // BATCH,),
         in_specs=[
-            pl.BlockSpec((BATCH, 64, LANES), lambda n: (n, 0, 0)),
+            pl.BlockSpec((BATCH, *sent), lambda n: (n, 0, 0)),
             whole(LANES, BJ),
             whole(1, BJ),
             whole(64, 1),
         ],
         out_specs=whole(60, BJ),
         out_shape=jax.ShapeDtypeStruct((60, BJ), jnp.float32),
-        scratch_shapes=[pltpu.VMEM((64, LANES), jnp.float32)],
+        scratch_shapes=[pltpu.VMEM(sent, jnp.float32)],
         compiler_params=pltpu.CompilerParams(vmem_limit_bytes=14 * MIB),
-        name="expand",
+        name="expand_narrow" if narrow else "expand",
     )(came, table, class_row, row_class)
 
 
 def on_device(amplitudes, integrals, a_irrep, b_irrep, virt_irrep, occ_irrep):
     virt, x, core = lax.axis_index("virt"), lax.axis_index("x"), lax.axis_index("c")
-    classes = (b_irrep[:, None] ^ occ_irrep[None, :]).reshape(BJ)
-    class_row, class_col = classes[None, :], classes[:, None]
-    a_rows = lax.dynamic_slice_in_dim(a_irrep, virt * 4, 4, 0)
-    i_rows = lax.dynamic_slice_in_dim(occ_irrep, (2 * x + core) * 15, 15, 0)
-    row_class = jnp.pad((i_rows[:, None] ^ a_rows[None, :]).reshape(60), (0, 4))[:, None]
-    fullest = jnp.max(jnp.sum(classes[:, None] == jnp.arange(8)[None, :], axis=0))
-
-    def one_pass(number):
+    labels = a_irrep, b_irrep, virt_irrep, occ_irrep
+
+    def contracted(number):
         first = (number * CAP).astype(jnp.int32)[None]
-        labels = a_irrep, b_irrep, virt_irrep, occ_irrep
-        send, weights = contract(False, first, *labels, amplitudes, integrals)
+        send, weights, fullest = contract(False, first, *labels, amplitudes, integrals)
         came = lax.ppermute(send, "c", [(0, 1), (1, 0)])
-        keep = contract(True, first, *labels, amplitudes, weights)
-        arrived = lax.all_to_all(merge(keep, came), ("virt", "x"), 0, 0, tiled=True)
-        table = make_table(first, class_row, class_col)
-        return expand(arrived, table, class_row, row_class)
-
-    passes = lax.div(fullest + (CAP - 1), CAP)
-    total = lax.fori_loop(1, passes, lambda n, total: total + one_pass(n), one_pass(jnp.int32(0)))
+        return first, *merge(contract(True, first, *labels, amplitudes, weights), came), fullest[0]
+
+    def finished(first, *coded):
+        classes = (b_irrep[:, None] ^ occ_irrep[None, :]).reshape(BJ)
+        class_row, class_col = classes[None, :], classes[:, None]
+        a_rows = lax.dynamic_slice_in_dim(a_irrep, virt * 4, 4, 0)
+        i_rows = lax.dynamic_slice_in_dim(occ_irrep, (2 * x + core) * 15, 15, 0)
+        row_class = jnp.pad((i_rows[:, None] ^ a_rows[None, :]).reshape(60), (0, 4))[:, None]
+        arrived = lax.all_to_all(jnp.concatenate(coded, axis=1), ("virt", "x"), 0, 0, tiled=True)
+        return expand(len(coded) == 1, arrived, make_table(first, class_row, class_col), class_row, row_class)
+
+    def all_passes(first, coded, more, fullest):
+        def one_pass(number, total):
+            first, coded, more, _ = contracted(number)
+            return total + finished(first, coded, more)
+
+        passes = lax.div(fullest + (CAP - 1), CAP)
+        return lax.fori_loop(1, passes, one_pass, finished(first, coded, more))
+
+    first, coded, more, fullest = contracted(jnp.int32(0))
+    total = lax.cond(
+        fullest <= 192,
+        lambda first, coded, more, fullest: finished(first, coded),
+        all_passes,
+        first, coded, more, fullest,
+    )
     return jnp.transpose(total.reshape(15, 4, BJ), (1, 0, 2))
 
 

time: 74.7 us -> 69.5 us (0.930)
  waiting for transfers between devices: 28.6 us -> 24.1 us
  Pallas kernels: 30.9 us -> 29.8 us
  local copies, waits for them, and re-layouts: 1.47 us -> 2.56 us
  other arithmetic: 0.91 us -> 0.15 us
    all_to_all x1, waiting for transfers between devices: 28.6 us -> 24.1 us  [finished(): lax.all_to_all(jnp.concatenate(coded, axis=1), ('virt', 'x'), 0, 0, tiled...]
    cond x0 -> x2, local copies, waits for them, and re-layouts: none -> 1.16 us
    pallas_call x1, Pallas kernels: 3.24 us -> 2.42 us  [merge(): pl.pallas_call(merge_kernel, grid=(4,), in_specs=[pl.BlockSpec((1, CODED,...]
  transfers between devices with their start and end apart: 2 -> 2, of which waited for: 1 -> 1; matrix products, arithmetic and copies ran while one was open for 2% -> 1% of each run, Pallas kernels for 17% -> 18%
where the time goes in v3:
time: 69.5 us; the launch traced here: 69.3 us
  Pallas kernels  29.8 us (43%)
  waiting for transfers between devices  24.1 us (35%)
  starting transfers between devices  11.6 us (17%)
  local copies, waits for them, and re-layouts  2.56 us (4%)
  between operations  0.74 us (1%)
    pallas_call x2, Pallas kernels, contract(): pl.pallas_call(functools.partial(contract_kernel, keeps), grid=(1,), in_s...  26 us
    all_to_all x1, waiting for transfers between devices, finished(): lax.all_to_all(jnp.concatenate(coded, axis=1), ('virt', 'x'), 0, 0, tiled...  24.1 us
    all_to_all x1, starting transfers between devices, finished(): lax.all_to_all(jnp.concatenate(coded, axis=1), ('virt', 'x'), 0, 0, tiled...  11.5 us
    pallas_call x1, Pallas kernels, merge(): pl.pallas_call(merge_kernel, grid=(4,), in_specs=[pl.BlockSpec((1, CODED,...  2.42 us
  transfers between devices with their start and end apart: 2, of which 1 were waited for; matrix products, arithmetic and copies ran while one was open for 1% of the time, Pallas kernels for 18%

profile of v3, /device:TPU:0, one launch (start us, length us, event | category | flops | bytes accessed | tf_op | source)
XLA Modules:
  0.0 69.3 jit_solution(10627000772468843296)
XLA Ops:
  0.0 0.0 copy-start.1
  0.0 0.0 copy-start.3
  0.0 0.0 copy-start.4
  0.0 0.0 copy-start.5
  0.0 14.1 %contract_send.4 = (s16[4,976,256]{2,1,0:T(8,128)(2,1)}, bf16[1024,256]{1,0:T(8,128)(2,1)S(1)}, s32[1]{0:T(128)}) custom-call(s32[1]{0:T(128)} %constant.77.clone.1.first, s32[64]{0:T(128)} %a_s.3, s32[8]{0:T(128)} %b_s.3, s32[1024]{0:T(1024)} %virt_s.3, s32[120]{0:T(128)} %occ_s.3, bf16[64,8,14400]{2,1,0:T(8,128)(2,1)} %last.3, bf16[64,8,14400]{2,1,0:T(8,128)(2,1)} %last.3, ...), custom_call_target="tpu_custom_call" | custom-call | flops 8000000000 | bytes 12000000 | tf_op jit(solution)/shard_map/contract_send/pallas_call | solution.py:168
  14.2 0.1 collective-permute-start.1
  14.9 0.0 copy-done.1
  14.9 0.0 copy-done.3
  14.9 0.0 copy-done.4
  14.9 0.0 copy-done.5
  14.9 11.9 %contract_keep.2.own = s16[4,976,256]{2,1,0:T(8,128)(2,1)S(1)} custom-call(s32[1]{0:T(128)} %constant.77.clone.1.first, s32[64]{0:T(128)S(1)} %copy-done.5, s32[8]{0:T(128)S(1)} %copy-done.4, s32[1024]{0:T(1024)S(1)} %copy-done.1, s32[120]{0:T(128)S(1)} %copy-done.3, bf16[64,8,14400]{2,1,0:T(8,128)(2,1)} %last.3, bf16[64,8,14400]{2,1,0:T(8,128)(2,1)} %last.3, ...), custom_call_target="tpu_custom_call" | custom-call | flops 8000000000 | bytes 12000000 | tf_op jit(solution)/shard_map/contract_keep/pallas_call | solution.py:168
  26.8 0.0 collective-permute-done.1.came
  26.9 2.4 %merge.4 = (s16[8,2,4,96,128]{4,3,2,1,0:T(8,128)(2,1)S(1)}, s16[8,2,4,32,128]{4,3,2,1,0:T(8,128)(2,1)S(1)}) custom-call(s16[4,976,256]{2,1,0:T(8,128)(2,1)S(1)} %contract_keep.2.own, s16[4,976,256]{2,1,0:T(8,128)(2,1)S(1)} %collective-permute-done.1.came), custom_call_target="tpu_custom_call" | custom-call | tf_op jit(solution)/shard_map/merge/pallas_call | solution.py:225
  29.3 39.2 %conditional.1 = (f32[60,960]{1,0:T(8,128)S(1)}) conditional(s32[]{:T(128)} %convert_element_type.3, (s16[8,2,4,32,128]{4,3,2,1,0:T(8,128)(2,1)S(1)}, s16[64,96,128]{2,1,0:T(8,128)(2,1)S(1)}, s32[8]{0:T(128)S(1)}, s32[120]{0:T(128)S(1)}, s32[]{:T(128)}, /*index=5*/s32[]{:T(128)}, s32[]{:T(128)}, s32[64]{0:T(128)S(1)}, s32[]{:T(128)}, s32[1024]{0:T(1024)}, ...), branch_computations={%region_0.3_spmd, %region_3.4_spmd} | conditional | flops 16002156544 | bytes 53718268 | solution.py:354
  29.5 0.0 copy-start
  29.5 1.2 %copy-done = s16[64,96,128]{2,1,0:T(8,128)(2,1)} copy-done((s16[64,96,128]{2,1,0:T(8,128)(2,1)}, s16[64,96,128]{2,1,0:T(8,128)(2,1)S(1)}, u32[]{:S(2)}) %copy-start) | copy-done | bytes 1572888 | tf_op jit(solution)/shard_map/cond
  30.7 11.5 %all-to-all-start = ((s16[64,96,128]{2,1,0:T(8,128)(2,1)}), s16[64,96,128]{2,1,0:T(8,128)(2,1)S(1)}, u32[]{:S(2)}, u32[]{:S(2)}) async-start(s16[64,96,128]{2,1,0:T(8,128)(2,1)} %copy-done), calls=%async_computation | async-start | bytes 3145728 | tf_op jit(solution)/shard_map/cond/branch_1_fun/all_to_all | solution.py:342
  42.2 0.1 broadcast_xor_fusion.5
  42.3 0.1 xor.150.class_row
  42.4 0.2 xor.158.class_col
  42.6 0.1 dynamic_slice.16
  42.6 0.1 dynamic_slice.17
  42.7 0.1 broadcast_xor_fusion.4
  42.8 0.1 xor.155
  42.9 0.1 copy.15.row_class
  43.0 0.5 table.6
  43.5 24.1 %all-to-all-done.came = s16[64,96,128]{2,1,0:T(8,128)(2,1)S(1)} async-done(((s16[64,96,128]{2,1,0:T(8,128)(2,1)}), s16[64,96,128]{2,1,0:T(8,128)(2,1)S(1)}, u32[]{:S(2)}, u32[]{:S(2)}) %all-to-all-start) | async-done | bytes 1572896 | tf_op jit(solution)/shard_map/cond/branch_1_fun/all_to_all | solution.py:342
  67.7 0.8 %expand_narrow.1 = f32[60,960]{1,0:T(8,128)S(1)} custom-call(s16[64,96,128]{2,1,0:T(8,128)(2,1)S(1)} %all-to-all-done.came, bf16[256,960]{1,0:T(8,128)(2,1)S(1)} %table.6, s32[1,960]{1,0:T(1,128)S(1)} %xor.150.class_row, s32[64,1]{1,0:T(8,128)S(1)} %copy.15.row_class), custom_call_target="tpu_custom_call" | custom-call | tf_op jit(solution)/shard_map/cond/branch_1_fun/expand_narrow/pallas_call | solution.py:309
  68.5 0.8 %reshape.195 = f32[15,4,960]{2,1,0:T(4,128)} reshape(f32[60,960]{1,0:T(8,128)S(1)} %get-tuple-element.361) | data formatting | bytes 460800 | tf_op jit(solution)/shard_map/reshape | solution.py:360
  (1 shorter events, 0.0 us)
Async XLA Ops:
  0.0 14.9 %copy-start.1 = (s32[1024]{0:T(1024)S(1)}, s32[1024]{0:T(1024)}, u32[]{:S(2)}) copy-start(s32[1024]{0:T(1024)} %virt_s.3) | copy-start | bytes 12292
  0.0 14.9 %copy-start.3 = (s32[120]{0:T(128)S(1)}, s32[120]{0:T(128)}, u32[]{:S(2)}) copy-start(s32[120]{0:T(128)} %occ_s.3) | copy-start | bytes 1444
  0.0 14.9 %copy-start.4 = (s32[8]{0:T(128)S(1)}, s32[8]{0:T(128)}, u32[]{:S(2)}) copy-start(s32[8]{0:T(128)} %b_s.3) | copy-start | bytes 100
  0.0 14.9 %copy-start.5 = (s32[64]{0:T(128)S(1)}, s32[64]{0:T(128)}, u32[]{:S(2)}) copy-start(s32[64]{0:T(128)} %a_s.3) | copy-start | bytes 772
  14.2 12.7 %collective-permute-start.1 = (s16[4,976,256]{2,1,0:T(8,128)(2,1)}, s16[4,976,256]{2,1,0:T(8,128)(2,1)S(1)}, u32[]{:S(2)}, u32[]{:S(2)}) collective-permute-start(s16[4,976,256]{2,1,0:T(8,128)(2,1)} %get-tuple-element.221), channel_id=1, source_target_pairs={{0,1},{1,0},{2,3},{3,2},{4,5},{5,4},{6,7},{7,6},{8,9},{9,8},{10,11... | collective-permute-start | bytes 5996552 | tf_op jit(solution)/shard_map/ppermute | solution.py:333
  29.5 1.2 %copy-start = (s16[64,96,128]{2,1,0:T(8,128)(2,1)}, s16[64,96,128]{2,1,0:T(8,128)(2,1)S(1)}, u32[]{:S(2)}) copy-start(s16[64,96,128]{2,1,0:T(8,128)(2,1)S(1)} %get-tuple-element.207) | copy-start | bytes 4718596 | tf_op jit(solution)/shard_map/cond
  30.7 37.0 %all-to-all-start = ((s16[64,96,128]{2,1,0:T(8,128)(2,1)}), s16[64,96,128]{2,1,0:T(8,128)(2,1)S(1)}, u32[]{:S(2)}, u32[]{:S(2)}) async-start(s16[64,96,128]{2,1,0:T(8,128)(2,1)} %copy-done), calls=%async_computation | async-start | bytes 3145728 | tf_op jit(solution)/shard_map/cond/branch_1_fun/all_to_all | solution.py:342
